TPU v7x, 256 devices: a whole 4x4x8 slice. The times are simulated.
256 devices in a mesh: batch: 8 (over x_hi, y), prefix: 32 (over z, x_lo, core).
Axes of the slice: x: 4 (x_hi: 2, x_lo: 2; x = x_hi * 2 + x_lo), y: 4, z: 8, core: 2. Of those that a mesh axis runs over, the one named last changes fastest.
Arguments:
- queries: bfloat16 [32, 128, 8192], P('batch', None, 'prefix'), may hold values from -32 to 32
- prompt_key_cache: bfloat16 [16384, 1024], P('prefix'), may hold values from -10 to 10
- prompt_value_cache: bfloat16 [16384, 1024], P('prefix'), may hold values from -12 to 12
- response_keys: bfloat16 [32, 128, 1024], P('batch'), may hold values from -10 to 10
- response_values: bfloat16 [32, 128, 1024], P('batch'), may hold values from -12 to 12
- lengths: int32 [32], P('batch'), may hold values from 32 to 128, as said below
- out_weight: bfloat16 [8192, 5120], P('prefix', 'batch'), may hold values from -0.0625 to 0.0625
Outputs:
- scored: bfloat16 [4096, 5120], P(('batch', 'prefix'))
Inputs may be any that keep to these rules, and one draw needn't show every extreme that they name: `lengths`: some response in every draw has all 128 tokens valid.
All inputs are finite; a program needn't handle non-finite values.
Results may differ from a plain program's by a relative error of at most 0.0052.
Values may be sent and summed in bfloat16 or wider, within the bound.
No kernel may reach another device: no remote copies, remote signals or barrier semaphores. Data moves between devices by JAX's collectives and lax.ppermute only.
A program may use at most 128 MiB of HBM per device.

v0:
```python
import jax
import jax.numpy as jnp
from jax import lax
from jax.sharding import PartitionSpec as P

QUERY_HEADS = 64
KEY_VALUE_HEADS = 8
HEAD_SIZE = 128


def block_partials(scores, values, equation):
    block_maximum = scores.max(-1)
    weights = jnp.exp(scores - block_maximum[..., None])
    running_sums = weights.sum(-1)
    summed = jnp.einsum(
        equation, weights.astype(jnp.bfloat16), values, preferred_element_type=jnp.float32
    )
    return ((summed / running_sums[..., None]).astype(jnp.bfloat16), block_maximum, running_sums)


def on_device(
    queries,
    prompt_key_cache,
    prompt_value_cache,
    response_keys,
    response_values,
    lengths,
    out_weight,
):
    position = lax.axis_index("prefix")
    resp_count, resp_len = (queries.shape[0], queries.shape[1])
    per_device = queries.shape[2] // HEAD_SIZE
    heads_per_group = QUERY_HEADS // KEY_VALUE_HEADS
    token_count = resp_count * resp_len
    score_scale = HEAD_SIZE ** (-0.5)
    kv_group = position * per_device // heads_per_group
    block_length = prompt_key_cache.shape[0]
    own_queries = queries.reshape(token_count, per_device, HEAD_SIZE)
    every_query_row = lax.all_gather(own_queries, "prefix", axis=1, tiled=True).reshape(
        token_count, KEY_VALUE_HEADS, heads_per_group, HEAD_SIZE
    )
    key_matrix = prompt_key_cache.reshape(block_length, KEY_VALUE_HEADS, HEAD_SIZE)
    value_matrix = prompt_value_cache.reshape(block_length, KEY_VALUE_HEADS, HEAD_SIZE)

    def group_queries(group_id):
        query_part = lax.dynamic_index_in_dim(every_query_row, group_id, 1, keepdims=False)
        key_part = lax.dynamic_index_in_dim(key_matrix, group_id, 1, keepdims=False)
        value_part = lax.dynamic_index_in_dim(value_matrix, group_id, 1, keepdims=False)
        scores = (
            jnp.einsum("trd,pd->trp", query_part, key_part, preferred_element_type=jnp.float32)
            * score_scale
        )
        return block_partials(scores, value_part, "trp,pd->trd")

    block_output, block_maximum, running_sums = lax.map(group_queries, jnp.arange(KEY_VALUE_HEADS))
    block_output = jnp.moveaxis(block_output, 0, 1).reshape(1, token_count, QUERY_HEADS, HEAD_SIZE)
    block_maximum = jnp.moveaxis(block_maximum, 0, 1).reshape(1, token_count, QUERY_HEADS)
    running_sums = jnp.moveaxis(running_sums, 0, 1).reshape(1, token_count, QUERY_HEADS)
    recv_out = lax.all_to_all(block_output, "prefix", split_axis=2, concat_axis=0, tiled=True)
    recv_top, recv_total = (
        lax.all_to_all(block_maximum, "prefix", split_axis=2, concat_axis=0, tiled=True),
        lax.all_to_all(running_sums, "prefix", split_axis=2, concat_axis=0, tiled=True),
    )
    prefix_top = recv_top.max(0)
    weight = recv_total * jnp.exp(recv_top - prefix_top)
    prefix_total = weight.sum(0)

    def add_member(member_id, running):
        member_out = lax.dynamic_index_in_dim(recv_out, member_id, 0, keepdims=False).astype(
            jnp.float32
        )
        member_weight = lax.dynamic_index_in_dim(weight, member_id, 0, keepdims=False)
        return running + member_weight[..., None] * member_out

    prefix_sum = lax.fori_loop(
        0,
        recv_out.shape[0],
        add_member,
        jnp.zeros((token_count, per_device, HEAD_SIZE), jnp.float32),
    )
    suffix_key = lax.dynamic_slice_in_dim(response_keys, kv_group * HEAD_SIZE, HEAD_SIZE, 2)
    suffix_value = lax.dynamic_slice_in_dim(response_values, kv_group * HEAD_SIZE, HEAD_SIZE, 2)
    query_resp = queries.reshape(resp_count, resp_len, per_device, HEAD_SIZE)
    scores = (
        jnp.einsum("bthd,bjd->bthj", query_resp, suffix_key, preferred_element_type=jnp.float32)
        * score_scale
    )
    causal = jnp.arange(resp_len)[:, None] >= jnp.arange(resp_len)[None, :]
    scores = jnp.where(causal[None, :, None, :], scores, -jnp.inf)
    suffix_top = scores.max(-1)
    suffix_prob = jnp.exp(scores - suffix_top[..., None])
    suffix_total = suffix_prob.sum(-1)
    suffix_out = (
        jnp.einsum(
            "bthj,bjd->bthd",
            suffix_prob.astype(jnp.bfloat16),
            suffix_value,
            preferred_element_type=jnp.float32,
        )
        / suffix_total[..., None]
    )
    suffix_top = suffix_top.reshape(token_count, per_device)
    suffix_total = suffix_total.reshape(token_count, per_device)
    suffix_out = suffix_out.reshape(token_count, per_device, HEAD_SIZE)
    overall = jnp.maximum(prefix_top, suffix_top)
    prefix_scale = jnp.exp(prefix_top - overall)
    suffix_scale = suffix_total * jnp.exp(suffix_top - overall)
    numerator = prefix_sum * prefix_scale[..., None] + suffix_scale[..., None] * suffix_out
    denominator = prefix_total * prefix_scale + suffix_scale
    live_rows = (jnp.arange(resp_len)[None, :] < lengths[:, None]).reshape(token_count)
    attended = (numerator / denominator[..., None]).reshape(token_count, per_device * HEAD_SIZE)
    attended = jnp.where(live_rows[:, None], attended, 0.0).astype(jnp.bfloat16)
    full_weight = lax.all_gather(out_weight, "batch", axis=1, tiled=True)
    return lax.psum_scatter(
        jnp.dot(attended, full_weight, preferred_element_type=jnp.float32),
        "prefix",
        scatter_dimension=0,
        tiled=True,
    ).astype(jnp.bfloat16)


def solution(mesh):
    placed = (
        P("batch", None, "prefix"),
        P("prefix", None),
        P("prefix", None),
        P("batch", None, None),
        P("batch", None, None),
        P("batch"),
        P("prefix", "batch"),
    )
    return jax.shard_map(
        on_device,
        mesh=mesh,
        in_specs=placed,
        out_specs=P(("batch", "prefix"), None),
        check_vma=False,
    )
```

profile of v0, /device:TPU:1, one launch (start us, length us, event | category | flops | bytes accessed | tf_op | source)
XLA Modules:
  0.0 645.6 jit_solution(14392538722131233045)
XLA Ops:
  12.3 74.3 %all-gather.3.cloned.1.call-done = bf16[512,64,128]{2,0,1:T(8,128)(2,1)} async-done(((bf16[512,2,128]{2,0,1:T(8,128)(2,1)}), bf16[512,64,128]{2,0,1:T(8,128)(2,1)}) %all-gather.3.cloned.1.call-update) | async-done | bytes 8388624 | tf_op jit(solution)/shard_map/all_gather | solution.py:39
  86.6 75.4 %while.28 = (s32[]{:T(128)}, bf16[8,512,8,128]{3,1,2,0:T(8,128)(2,1)}, f32[8,512,8]{1,2,0:T(8,128)S(1)}, f32[8,512,8]{1,2,0:T(8,128)S(1)}, s32[8]{0:T(128)S(1)},...) while((s32[]{:T(128)}, ...), condition=%wide.region_3.4_spmd, body=%wide.region_0.3_spmd.sunk | while | flops 1091559424 | bytes 27674276 | solution.py:55
  89.1 2.5 multiply_reduce_fusion.2
  93.1 3.0 bitcast_dynamic-update-slice_fusion.5
  98.6 2.5 multiply_reduce_fusion.2
  102.5 2.9 bitcast_dynamic-update-slice_fusion.5
  108.0 2.5 multiply_reduce_fusion.2
  111.9 2.9 bitcast_dynamic-update-slice_fusion.5
  117.4 2.5 multiply_reduce_fusion.2
  121.3 2.9 bitcast_dynamic-update-slice_fusion.5
  126.8 2.5 multiply_reduce_fusion.2
  130.7 3.0 bitcast_dynamic-update-slice_fusion.5
  140.2 2.9 bitcast_dynamic-update-slice_fusion.5
  149.6 3.0 bitcast_dynamic-update-slice_fusion.5
  155.1 2.5 multiply_reduce_fusion.2
  159.1 2.9 bitcast_dynamic-update-slice_fusion.5
  162.8 6.3 all-to-all-start.1
  169.2 9.1 %all-to-all-done.1 = f32[1,512,64]{1,0,2:T(1,128)S(1)} async-done(((f32[1,512,64]{1,0,2:T(1,128)}), f32[1,512,64]{1,0,2:T(1,128)S(1)}, u32[]{:S(2)}, u32[]{:S(2)}) %all-to-all-start.1) | async-done | bytes 131104 | tf_op jit(solution)/shard_map/all_to_all | solution.py:61
  178.3 12.5 %all_to_all.54 = f32[1,512,64]{1,0,2:T(1,128)S(1)} all-to-all(f32[1,512,64]{1,0,2:T(1,128)S(1)} %copy.68), channel_id=1, replica_groups=mesh['batch'=8,'prefix'=32] {'prefix'}, dimensions={2} | all-to-all | bytes 262144 | tf_op jit(solution)/shard_map/all_to_all | solution.py:62
  190.9 5.2 all-to-all-start.2
  198.8 184.0 %all-to-all-done.2 = bf16[1,512,64,128]{3,1,0,2:T(8,128)(2,1)} async-done(((bf16[1,512,64,128]{3,1,0,2:T(8,128)(2,1)}), bf16[1,512,64,128]{3,1,0,2:T(8,128)(2,1)}, u32[]{:S(2)}, u32[]{:S(2)}) %all-to-all-start.2) | async-done | bytes 8388640 | tf_op jit(solution)/shard_map/all_to_all | solution.py:59
  382.8 116.6 %while.29 = (s32[]{:T(128)}, f32[512,2,128]{2,1,0:T(2,128)S(1)}, f32[32,512,2]{1,2,0:T(2,128)S(1)}, bf16[32,512,2,128]{3,1,2,0:T(8,128)(2,1)}, s32[]{:T(128)}, /*index=5*/s32[]{:T(128)}) while((s32[]{:T(128)}, f32[512,2,128]{2,1,0:T(2,128)S(1)}, f32[32,512,2]{1,2,0:T(2,128)S(1)}, bf16[32,512,2,128]{3,1,2,0:T(8,128)(2,1)}, ...), condition=%wide.region_6.7_spmd.clone, body=%wide.region_5.6_spmd.clone.sunk | while | flops 524291 | bytes 1855575 | solution.py:75
  500.2 7.3 %fusion.45 = f32[512,5120]{1,0:T(8,128)} fusion(bf16[512,256]{0,1:T(8,128)(2,1)S(1)} %fusion.21, bf16[256,5120]{1,0:T(8,128)(2,1)} %all-gather.5.cloned.1.call-done), kind=kOutput, calls=%fused_computation.63 | convolution fusion | flops 1342177280 | bytes 13369344 | tf_op jit(solution)/shard_map/dot_general | solution.py:115
  507.5 129.0 %reduce-scatter.2.cloned.1.call-done = f32[16,5120]{1,0:T(8,128)} async-done(((f32[512,5120]{1,0:T(8,128)}), f32[16,5120]{1,0:T(8,128)}) %reduce-scatter.2.cloned.1.call-update) | async-done | bytes 327696 | tf_op jit(solution)/shard_map/reduce_scatter | solution.py:114
  (191 shorter events, 147.0 us)
Async XLA Ops:
  7.4 189.5 %copy-start = (bf16[4,128,1024]{2,1,0:T(8,128)(2,1)S(1)}, bf16[4,128,1024]{2,1,0:T(8,128)(2,1)}, u32[]{:S(2)}) copy-start(bf16[4,128,1024]{2,1,0:T(8,128)(2,1)} %param.14) | copy-start | bytes 3145732
  7.4 79.2 %all-gather.3.cloned.1.call-start = ((), (), s32[]{:S(2)}) async-start(), calls=%async_computation.4 | async-start | bytes 8650752 | tf_op jit(solution)/shard_map/all_gather | solution.py:39
  162.8 15.5 %all-to-all-start.1 = ((f32[1,512,64]{1,0,2:T(1,128)}), f32[1,512,64]{1,0,2:T(1,128)S(1)}, u32[]{:S(2)}, u32[]{:S(2)}) async-start(f32[1,512,64]{1,0,2:T(1,128)} %copy.69), calls=%async_computation.1 | async-start | bytes 262144 | tf_op jit(solution)/shard_map/all_to_all | solution.py:61
  190.9 6.0 copy-start.1
  190.9 7.6 %copy-start.2 = (s32[4]{0:T(128)S(1)}, s32[4]{0:T(128)}, u32[]{:S(2)}) copy-start(s32[4]{0:T(128)} %param.16) | copy-start | bytes 52
  190.9 191.9 %all-to-all-start.2 = ((bf16[1,512,64,128]{3,1,0,2:T(8,128)(2,1)}), bf16[1,512,64,128]{3,1,0,2:T(8,128)(2,1)}, u32[]{:S(2)}, u32[]{:S(2)}) async-start(bf16[1,512,64,128]{3,1,0,2:T(8,128)(2,1)} %bitcast.23), calls=%async_computation.2 | async-start | bytes 16777216 | tf_op jit(solution)/shard_map/all_to_all | solution.py:59
  196.1 304.1 %all-gather.5.cloned.1.call-start = ((), (), s32[]{:S(2)}) async-start(), calls=%async_computation.5 | async-start | bytes 2949120 | tf_op jit(solution)/shard_map/all_gather | solution.py:113
  196.7 439.8 %reduce-scatter.2.cloned.1.call-start = ((), (), s32[]{:S(2)}) async-start(), calls=%async_computation.6 | async-start | bytes 10813440 | tf_op jit(solution)/shard_map/reduce_scatter | solution.py:114
Sparse Core Ops, SparseCore 0:
  10.0 76.4 all-gather.2
  507.6 128.8 reduce-scatter.1
Sparse Core Ops, SparseCore 1:
  199.3 86.1 all-gather.4
where the time goes:
time: 650 us; the launch traced here: 646 us
  waiting for transfers between devices  397 us (61%)
  other arithmetic  92.8 us (14%)
  matrix products  52.7 us (8%)
  local copies, waits for them, and re-layouts  47 us (7%)
  loops' own time  16.9 us (3%)
  between operations  15 us (2%)
  blocking collectives  12.5 us (2%)
  starting transfers between devices  11.6 us (2%)
    all_to_all x1, waiting for transfers between devices, on_device(): lax.all_to_all(block_output, 'prefix', split_axis=2, concat_axis=0, tiled...  184 us
    reduce_scatter x1, waiting for transfers between devices, on_device(): lax.psum_scatter(jnp.dot(attended, full_weight, preferred_element_type=jn...  129 us
    add x32, other arithmetic, add_member(): return running + member_weight[..., None] * member_out  79.1 us
    all_gather x1, waiting for transfers between devices, on_device(): lax.all_gather(own_queries, 'prefix', axis=1, tiled=True)  74.3 us
    dynamic_slice x32, local copies, waits for them, and re-layouts, add_member(): lax.dynamic_index_in_dim(recv_out, member_id, 0, keepdims=False)  31.2 us
    dot_general x8, matrix products, block_partials(): jnp.einsum(equation, weights.astype(jnp.bfloat16), values, preferred_elem...  23.6 us
    dot_general x8, matrix products, group_queries(): jnp.einsum('trd,pd->trp', query_part, key_part, preferred_element_type=jn...  20.3 us
    another operation x1, loops' own time, on_device(): lax.map(group_queries, jnp.arange(KEY_VALUE_HEADS))  15.5 us
  transfers between devices with their start and end apart: 5, of which 4 were waited for; matrix products, arithmetic and copies ran while one was open for 19% of the time, Pallas kernels for 0%

commit v1 on v0

v1 whole, which is shorter than its diff:
```python
import functools
import math

import jax
import jax.numpy as jnp
from jax import lax
from jax.experimental import pallas as pl
from jax.experimental.pallas import tpu as pltpu
from jax.sharding import Mesh, PartitionSpec as P

HEAD_SIZE = 128
F32 = jnp.float32
BF16 = jnp.bfloat16
SCORE_SCALE = HEAD_SIZE**-0.5 * math.log2(math.e)
LOWEST = -1e30
VMEM_LIMIT = 40 * 2**20
SUB_AXES = ("xh", "y", "z", "xl", "c")
PREFIX = ("z", "xl", "c")
SWAP = [(0, 1), (1, 0)]


def score_dot(q, k):
    return lax.dot_general(q, k, (((1,), (1,)), ((), ())), preferred_element_type=F32)


def absorb(state, scores, values):
    top, total, acc = state
    new_top = jnp.maximum(top, scores.max(-1, keepdims=True) * SCORE_SCALE)
    decay = jnp.exp2(top - new_top)
    weights = jnp.exp2(scores * SCORE_SCALE - new_top).astype(BF16)
    extended = jnp.concatenate([values, jnp.ones(values.shape, BF16)], axis=1)
    added = jnp.dot(weights, extended, preferred_element_type=F32)
    return new_top, total * decay + added[:, 128:129], acc * decay + added[:, :128]


def empty_state(rows):
    return (
        jnp.full((rows, 1), LOWEST, F32),
        jnp.zeros((rows, 1), F32),
        jnp.zeros((rows, HEAD_SIZE), F32),
    )


def store_state(state, acc_out, stat_out):
    top, total, acc = state
    acc_out[...] = acc
    lane = lax.broadcasted_iota(jnp.int32, acc.shape, 1)
    stat_out[...] = jnp.where(lane < 64, top, total)


def absorb_blocks(state, q, blocks, chunk):
    for block in blocks:
        for at in range(0, block.shape[1], chunk):
            keys = block[0, at : at + chunk, :]
            values = block[1, at : at + chunk, :]
            state = absorb(state, score_dot(q, keys), values)
    return state


def first_own_kernel(chunk, q_ref, rk_ref, rv_ref, block, acc_out, stat_out):
    resp_len = rk_ref.shape[1]
    row = lax.broadcasted_iota(jnp.int32, (resp_len, resp_len), 0)
    col = lax.broadcasted_iota(jnp.int32, (resp_len, resp_len), 1)
    tops, totals, accs = [], [], []
    for r in range(rk_ref.shape[0]):
        q = q_ref[r * resp_len : (r + 1) * resp_len, :]
        scores = jnp.where(row >= col, score_dot(q, rk_ref[r]), LOWEST)
        top, total, acc = absorb(empty_state(resp_len), scores, rv_ref[r])
        tops.append(top)
        totals.append(total)
        accs.append(acc)
    state = tuple(jnp.concatenate(part, axis=0) for part in (tops, totals, accs))
    state = absorb_blocks(state, q_ref[...], [block], chunk)
    store_state(state, acc_out, stat_out)


def first_other_kernel(chunk, q_ref, block, acc_in, stat_in, acc_out, stat_out):
    del acc_in, stat_in
    state = absorb_blocks(empty_state(q_ref.shape[0]), q_ref[...], [block], chunk)
    store_state(state, acc_out, stat_out)


def middle_kernel(chunk, count, q_ref, *refs):
    blocks, (acc_in, stat_in, acc_out, stat_out) = refs[:count], refs[count:]
    state = (stat_in[:, 0:1], stat_in[:, 64:65], acc_in[...])
    state = absorb_blocks(state, q_ref[...], blocks, chunk)
    store_state(state, acc_out, stat_out)


def last_kernel(chunk, count, q_ref, *refs):
    blocks, (acc_in, stat_in, out_ref, lse_ref) = refs[:count], refs[count:]
    state = (stat_in[:, 0:1], stat_in[:, 64:65], acc_in[...])
    top, total, acc = absorb_blocks(state, q_ref[...], blocks, chunk)
    out_ref[...] = (acc / total).astype(BF16)
    lse = top + jnp.log2(total)
    lse_ref[...] = jnp.broadcast_to(lse, acc.shape).T[0:8]


def attention_cost(rows, positions):
    return pl.CostEstimate(
        flops=8 * rows * positions * HEAD_SIZE,
        bytes_accessed=rows * 2048,
        transcendentals=rows * positions,
    )


def params():
    return pltpu.CompilerParams(vmem_limit_bytes=VMEM_LIMIT)


def whole(array):
    return pl.BlockSpec(array.shape, lambda i: (0,) * array.ndim)


def rows_spec(tile, offset=0):
    return pl.BlockSpec((tile, HEAD_SIZE), lambda i: (i + offset, 0))


def first_own(q, resp_k, resp_v, block, all_rows, tile, chunk):
    rows = q.shape[0]
    state = jax.ShapeDtypeStruct((all_rows, HEAD_SIZE), F32)
    return pl.pallas_call(
        functools.partial(first_own_kernel, chunk),
        grid=(rows // tile,),
        in_specs=[rows_spec(tile), whole(resp_k), whole(resp_v), whole(block)],
        out_specs=[rows_spec(tile)] * 2,
        out_shape=[state] * 2,
        cost_estimate=attention_cost(rows, block.shape[1]),
        compiler_params=params(),
        name="attend_own",
    )(q, resp_k, resp_v, block)


def first_other(q, block, state, start, tile, chunk):
    rows = q.shape[0]
    at = start // tile
    return pl.pallas_call(
        functools.partial(first_other_kernel, chunk),
        grid=(rows // tile,),
        in_specs=[rows_spec(tile), whole(block)] + [pl.BlockSpec(memory_space=pl.ANY)] * 2,
        out_specs=[rows_spec(tile, at)] * 2,
        out_shape=[jax.ShapeDtypeStruct(s.shape, s.dtype) for s in state],
        input_output_aliases={2: 0, 3: 1},
        cost_estimate=attention_cost(rows, block.shape[1]),
        compiler_params=params(),
        name="attend_first",
    )(q, block, *state)


def more(q, blocks, state, last, tile, chunk):
    rows = q.shape[0]
    count = len(blocks)
    if last:
        kernel = last_kernel
        out_specs = [rows_spec(tile), pl.BlockSpec((8, tile), lambda i: (0, i))]
        out_shape = [
            jax.ShapeDtypeStruct((rows, HEAD_SIZE), BF16),
            jax.ShapeDtypeStruct((8, rows), F32),
        ]
        aliases = {}
    else:
        kernel = middle_kernel
        out_specs = [rows_spec(tile)] * 2
        out_shape = [jax.ShapeDtypeStruct(s.shape, s.dtype) for s in state]
        aliases = {1 + count: 0, 2 + count: 1}
    return pl.pallas_call(
        functools.partial(kernel, chunk, count),
        grid=(rows // tile,),
        in_specs=[rows_spec(tile)] + [whole(b) for b in blocks] + [rows_spec(tile)] * 2,
        out_specs=out_specs,
        out_shape=out_shape,
        input_output_aliases=aliases,
        cost_estimate=attention_cost(rows, sum(b.shape[1] for b in blocks)),
        compiler_params=params(),
        name="attend_last" if last else "attend_more",
    )(q, *blocks, *state)


def pack_kernel(z_ref, k_ref, v_ref, *outs):
    groups = len(outs)
    for d in range(groups):
        group = lax.rem(z_ref[0] + d, groups)
        columns = pl.ds(pl.multiple_of(group * HEAD_SIZE, HEAD_SIZE), HEAD_SIZE)
        outs[d][0] = k_ref[:, columns]
        outs[d][1] = v_ref[:, columns]


def pack(z, keys, values):
    groups = keys.shape[1] // HEAD_SIZE
    out = jax.ShapeDtypeStruct((2, keys.shape[0], HEAD_SIZE), BF16)
    return pl.pallas_call(
        pack_kernel,
        in_specs=[
            pl.BlockSpec(memory_space=pltpu.SMEM),
            pl.BlockSpec(memory_space=pltpu.VMEM),
            pl.BlockSpec(memory_space=pltpu.VMEM),
        ],
        out_specs=[pl.BlockSpec(memory_space=pltpu.VMEM)] * groups,
        out_shape=[out] * groups,
        compiler_params=params(),
        name="pack_heads",
    )(z.reshape(1), keys, values)


def column(lse):
    return jnp.broadcast_to(lse[0:1], (HEAD_SIZE, lse.shape[1])).T


def merge(out_a, lse_a, out_b, lse_b):
    top = jnp.maximum(lse_a, lse_b)
    weight_a, weight_b = jnp.exp2(lse_a - top), jnp.exp2(lse_b - top)
    total = weight_a + weight_b
    merged = (weight_a * out_a.astype(F32) + weight_b * out_b.astype(F32)) / total
    return merged, top + jnp.log2(total)


def merge_kernel(a_ref, a_lse, b_ref, b_lse, out_ref, lse_ref):
    out, lse = merge(a_ref[...], column(a_lse), b_ref[...], column(b_lse))
    out_ref[...] = out.astype(BF16)
    lse_ref[...] = lse.T[0:8]


def final_merge_kernel(a_ref, a_lse, b_ref, b_lse, live_ref, out_ref):
    out, _ = merge(a_ref[...], column(a_lse), b_ref[...], column(b_lse))
    out_ref[...] = jnp.where(column(live_ref) > 0, out, 0.0).astype(BF16)


def merge_pair(own, other, rows, tile):
    out_spec = rows_spec(tile)
    lse_spec = pl.BlockSpec((8, tile), lambda i: (0, i))
    return pl.pallas_call(
        merge_kernel,
        grid=(rows // tile,),
        in_specs=[out_spec, lse_spec] * 2,
        out_specs=[out_spec, lse_spec],
        out_shape=[
            jax.ShapeDtypeStruct((rows, HEAD_SIZE), BF16),
            jax.ShapeDtypeStruct((8, rows), F32),
        ],
        compiler_params=params(),
        name="merge_pair",
    )(*own, *other)


def merge_final(own, other, live):
    rows = own[0].shape[0]
    tokens = live.shape[1]
    blocks = rows // tokens
    out_spec = pl.BlockSpec((tokens, HEAD_SIZE), lambda i: (i, 0))
    lse_spec = pl.BlockSpec((8, tokens), lambda i: (0, i))
    half = blocks // 2
    out_turned = pl.BlockSpec((tokens, HEAD_SIZE), lambda i: ((i + half) % blocks, 0))
    lse_turned = pl.BlockSpec((8, tokens), lambda i: (0, (i + half) % blocks))
    return pl.pallas_call(
        final_merge_kernel,
        grid=(blocks,),
        in_specs=[out_spec, lse_spec, out_turned, lse_turned, whole(live)],
        out_specs=pl.BlockSpec((tokens, HEAD_SIZE), lambda i: (0, i)),
        out_shape=jax.ShapeDtypeStruct((tokens, blocks * HEAD_SIZE), BF16),
        compiler_params=params(),
        name="merge_final",
    )(*own, *other, live)


def on_device(queries, keys, values, resp_keys, resp_values, lengths, out_weight):
    z, xl, c = (lax.axis_index(a) for a in PREFIX)
    resp_count, resp_len, features = queries.shape
    tokens = resp_count * resp_len
    tile, chunk = 512, 256
    z_size = lax.axis_size("z")

    own_heads = features // HEAD_SIZE
    own_rows = own_heads * tokens
    q_own = queries.reshape(tokens, own_heads, HEAD_SIZE)
    q_own = jnp.moveaxis(q_own, 1, 0).reshape(own_rows, HEAD_SIZE)
    q_x = lax.ppermute(q_own, "xl", SWAP)
    q_c = lax.ppermute(q_own, "c", SWAP)
    q_xc = lax.ppermute(q_x, "c", SWAP)

    packed = pack(z, keys, values)
    blocks = [packed[0]]
    for d in range(1, z_size):
        blocks.append(lax.ppermute(packed[d], "z", [(i, (i + d) % z_size) for i in range(z_size)]))

    depth, width = out_weight.shape
    quarters = out_weight.T.reshape(2, 2, width // 4, depth)
    of_c = lax.dynamic_index_in_dim(quarters, c, 1, keepdims=False)
    from_c = lax.ppermute(
        lax.dynamic_index_in_dim(quarters, 1 - c, 1, keepdims=False), "c", SWAP
    )
    both = jnp.stack([of_c, from_c], axis=1)
    mine = lax.dynamic_index_in_dim(both, xl, 0, keepdims=False)
    theirs = lax.ppermute(lax.dynamic_index_in_dim(both, 1 - xl, 0, keepdims=False), "xl", SWAP)
    weight_part = jnp.stack([mine[0], theirs[0], mine[1], theirs[1]], axis=1)
    weight_part = weight_part.reshape(width // 4, 4 * depth)
    weight = lax.all_gather(weight_part, ("xh", "y"), axis=0, tiled=True)

    head = z * HEAD_SIZE
    rk = lax.dynamic_slice_in_dim(resp_keys, head, HEAD_SIZE, 2)
    rv = lax.dynamic_slice_in_dim(resp_values, head, HEAD_SIZE, 2)

    state = first_own(q_own, rk, rv, blocks[0], 4 * own_rows, tile, chunk)
    q_rest = jnp.concatenate([q_x, q_c, q_xc], axis=0)
    state = first_other(q_rest, blocks[0], state, own_rows, tile, chunk)
    q_all = jnp.concatenate([q_own, q_rest], axis=0)
    state = more(q_all, [blocks[1], blocks[7]], state, False, tile, chunk)
    state = more(q_all, [blocks[2], blocks[6]], state, False, tile, chunk)
    out, lse = more(q_all, [blocks[3], blocks[5], blocks[4]], state, True, tile, chunk)

    half = 2 * own_rows
    sent = (lax.ppermute(out[half:], "c", SWAP), lax.ppermute(lse[:, half:], "c", SWAP))
    out, lse = merge_pair((out, lse), sent, half, tile)
    sent = (lax.ppermute(out, "xl", SWAP), lax.ppermute(lse, "xl", SWAP))
    live = (jnp.arange(resp_len)[None, :] < lengths[:, None]).astype(F32).reshape(1, tokens)
    live = jnp.broadcast_to(live, (8, tokens))
    attended = merge_final((out, lse), sent, live)
    attended_c = lax.ppermute(attended, "c", SWAP)

    depth_half = 2 * depth
    contract = (((1,), (1,)), ((), ()))
    partial = lax.dot_general(
        attended, weight[:, :depth_half], contract, preferred_element_type=F32
    ) + lax.dot_general(attended_c, weight[:, depth_half:], contract, preferred_element_type=F32)
    partial = partial.astype(BF16)

    received = lax.all_to_all(partial, PREFIX, split_axis=0, concat_axis=0, tiled=True)
    out_rows = tokens // (z_size * 4)
    received = received.reshape(z_size, 4, out_rows, -1, width // 4)
    total = received.astype(F32).sum(0).astype(BF16)
    return total.transpose(1, 2, 0, 3).reshape(out_rows, -1)


def solution(mesh):
    shape = (2, mesh.shape["batch"] // 2, mesh.shape["prefix"] // 4, 2, 2)
    fine = Mesh(mesh.devices.reshape(shape), SUB_AXES)
    batch = ("xh", "y")
    placed = (
        P(batch, None, PREFIX),
        P(PREFIX, None),
        P(PREFIX, None),
        P(batch, None, None),
        P(batch, None, None),
        P(batch),
        P(PREFIX, batch),
    )
    return jax.shard_map(
        on_device,
        mesh=fine,
        in_specs=placed,
        out_specs=P(batch + PREFIX, None),
        check_vma=False,
    )
```

time: 650 us -> 308 us (0.47)
  waiting for transfers between devices: 397 us -> 39.8 us
  Pallas kernels: 0 us -> 168 us
  other arithmetic: 92.8 us -> 2.89 us
  matrix products: 52.7 us -> 3.22 us
  local copies, waits for them, and re-layouts: 47 us -> 10.8 us
  blocking collectives: 12.5 us -> 41.1 us
  loops' own time: 16.9 us -> 0 us
  starting transfers between devices: 11.6 us -> 27.9 us
    all_to_all x2 -> x0, waiting for transfers between devices: 193 us -> none  [the longest x1 184 us: on_device(): lax.all_to_all(block_output, 'prefix', split_axis=2, concat_axis=0, tiled...]
    pallas_call x0 -> x8, Pallas kernels: none -> 168 us  [the longest x3 155 us: more(): pl.pallas_call(functools.partial(kernel, chunk, count), grid=(rows // til...]
    reduce_scatter x1 -> x0, waiting for transfers between devices: 129 us -> none  [on_device(): lax.psum_scatter(jnp.dot(attended, full_weight, preferred_element_type=jn...]
    add x33 -> x0, other arithmetic: 79.1 us -> none  [the longest x32 79.1 us: add_member(): return running + member_weight[..., None] * member_out]
    all_gather x2 -> x1, waiting for transfers between devices: 74.3 us -> 0.01 us  [on_device(): weight = lax.all_gather(weight_part, ('xh', 'y'), axis=0, tiled=True)]
    dot_general x19 -> x2, matrix products: 52.7 us -> 3.22 us  [the longest x1 2.33 us: on_device(): lax.dot_general(attended_c, weight[:, depth_half:], contract, preferred_e...]
    dynamic_slice x104 -> x1, local copies, waits for them, and re-layouts: 40.9 us -> 0.99 us  [on_device(): rv = lax.dynamic_slice_in_dim(resp_values, head, HEAD_SIZE, 2)]
    ppermute x0 -> x17, waiting for transfers between devices: none -> 39.8 us  [the longest x2 13 us: on_device(): sent = (lax.ppermute(out, 'xl', SWAP), lax.ppermute(lse, 'xl', SWAP))]
  transfers between devices with their start and end apart: 5 -> 18, of which waited for: 4 -> 8; matrix products, arithmetic and copies ran while one was open for 19% -> 1% of each run, Pallas kernels for 0% -> 55%
where the time goes in v1:
time: 308 us; the launch traced here: 307 us
  Pallas kernels  168 us (55%)
  blocking collectives  41.1 us (13%)
  waiting for transfers between devices  39.8 us (13%)
  starting transfers between devices  27.9 us (9%)
  between operations  13.7 us (4%)
  local copies, waits for them, and re-layouts  10.8 us (4%)
  matrix products  3.22 us (1%)
    pallas_call x3, Pallas kernels, more(): pl.pallas_call(functools.partial(kernel, chunk, count), grid=(rows // til...  155 us
    all_to_all x1, blocking collectives, on_device(): lax.all_to_all(partial, PREFIX, split_axis=0, concat_axis=0, tiled=True)  41.1 us
    ppermute x7, starting transfers between devices, on_device(): lax.ppermute(packed[d], 'z', [(i, (i + d) % z_size) for i in range(z_size)])  16.8 us
    ppermute x2, waiting for transfers between devices, on_device(): sent = (lax.ppermute(out, 'xl', SWAP), lax.ppermute(lse, 'xl', SWAP))  13 us
    ppermute x7, waiting for transfers between devices, on_device(): lax.ppermute(packed[d], 'z', [(i, (i + d) % z_size) for i in range(z_size)])  12.1 us
  transfers between devices with their start and end apart: 18, of which 8 were waited for; matrix products, arithmetic and copies ran while one was open for 1% of the time, Pallas kernels for 55%

profile of v1, /device:TPU:1, one launch (start us, length us, event | category | flops | bytes accessed | tf_op | source)
XLA Modules:
  0.0 307.5 jit_solution(8292425376920295635)
XLA Ops:
  7.8 3.3 %collective-permute-start.14 = (bf16[2,160,256]{2,1,0:T(8,128)(2,1)S(1)}, bf16[2,160,256]{2,1,0:T(8,128)(2,1)S(1)}, u32[]{:S(2)}, u32[]{:S(2)}) collective-permute-start(bf16[2,160,256]{2,1,0:T(8,128)(2,1)S(1)} %get-tuple-element.47), channel_id=1, source_target_pairs={{0,1},{1,0},{2,3},{3,2},{4,5},{5,4},{6,7},{7,6},{8,9},{9,8},{10,11... | collective-permute-start | bytes 491528 | tf_op jit(solution)/shard_map/ppermute | solution.py:288
  12.3 5.4 %collective-permute-done.15 = bf16[2,160,256]{2,1,0:T(8,128)(2,1)S(1)} collective-permute-done((bf16[2,160,256]{2,1,0:T(8,128)(2,1)S(1)}, bf16[2,160,256]{2,1,0:T(8,128)(2,1)S(1)}, u32[]{:S(2)}, u32[]{:S(2)}) %collective-permute-start.15) | collective-permute-done | bytes 163872 | tf_op jit(solution)/shard_map/ppermute | solution.py:293
  20.2 5.2 %collective-permute-done = bf16[1024,128]{1,0:T(8,128)(2,1)} collective-permute-done((bf16[1024,128]{1,0:T(8,128)(2,1)S(1)}, bf16[1024,128]{1,0:T(8,128)(2,1)}, u32[]{:S(2)}, u32[]{:S(2)}) %collective-permute-start) | collective-permute-done | bytes 262176 | tf_op jit(solution)/shard_map/ppermute | solution.py:276
  25.5 2.1 collective-permute-start.2
  31.0 2.6 collective-permute-start.3
  33.6 2.1 collective-permute-start.4
  35.7 4.9 %collective-permute-start.5 = (bf16[2,512,128]{2,1,0:T(8,128)(2,1)S(1)}, bf16[2,512,128]{2,1,0:T(8,128)(2,1)S(1)}, u32[]{:S(2)}, u32[]{:S(2)}) collective-permute-start(bf16[2,512,128]{2,1,0:T(8,128)(2,1)S(1)} %get-tuple-element.27), channel_id=1, source_target_pairs={{0,16},{4,20},{8,24},{12,28},{16,0},{20,4},{24,8},{28,12},{1,17},{... | collective-permute-start | bytes 786440 | tf_op jit(solution)/shard_map/ppermute | solution.py:283
  42.6 5.8 %attend_own.1 = (f32[4096,128]{1,0:T(8,128)S(1)}, f32[4096,128]{1,0:T(8,128)S(1)}) custom-call(bf16[1024,128]{1,0:T(8,128)(2,1)S(1)} %bitcast.33, bf16[4,128,128]{2,1,0:T(8,128)(2,1)S(1)} %get-tuple-element.54.rk_ref, bf16[4,128,128]{2,1,0:T(8,128)(2,1)S(1)} %get-tuple-element.53.rv_ref, bf16[2,512,128]{2,1,0:T(8,128)(2,1)S(1)} %copy-done.9), custom_call_target="tpu_custom_call" | custom-call | flops 536870912 | bytes 2097152 | tf_op jit(solution)/shard_map/attend_own/pallas_call | solution.py:122
  49.3 1.9 collective-permute-start.9
  53.6 4.2 %attend_first.1 = (f32[4096,128]{1,0:T(8,128)S(1)}, f32[4096,128]{1,0:T(8,128)S(1)}) custom-call(bf16[3072,128]{1,0:T(8,128)(2,1)S(1)} %pad_maximum_fusion.1.q_ref, bf16[2,512,128]{2,1,0:T(8,128)(2,1)S(1)} %copy-done.9, f32[4096,128]{1,0:T(8,128)S(1)} %get-tuple-element.33.acc_in, ...), custom_call_target="tpu_custom_call", output_to_operand_aliasing={{0}: (2, {}), {1}: (3, {})} | custom-call | flops 1610612736 | bytes 6291456 | tf_op jit(solution)/shard_map/attend_first/pallas_call | solution.py:137
  57.8 11.8 %collective-permute-done.8.refs_0_ = bf16[2,512,128]{2,1,0:T(8,128)(2,1)S(1)} collective-permute-done((bf16[2,512,128]{2,1,0:T(8,128)(2,1)S(1)}, bf16[2,512,128]{2,1,0:T(8,128)(2,1)S(1)}, u32[]{:S(2)}, u32[]{:S(2)}) %collective-permute-start.8) | collective-permute-done | bytes 262176 | tf_op jit(solution)/shard_map/ppermute | solution.py:283
  69.6 1.3 collective-permute-start.6
  71.2 3.1 %collective-permute-start.7 = (bf16[2,512,128]{2,1,0:T(8,128)(2,1)S(1)}, bf16[2,512,128]{2,1,0:T(8,128)(2,1)S(1)}, u32[]{:S(2)}, u32[]{:S(2)}) collective-permute-start(bf16[2,512,128]{2,1,0:T(8,128)(2,1)S(1)} %get-tuple-element.29), channel_id=1, source_target_pairs={{0,24},{4,28},{8,0},{12,4},{16,8},{20,12},{24,16},{28,20},{1,25},{... | collective-permute-start | bytes 786440 | tf_op jit(solution)/shard_map/ppermute | solution.py:283
  74.3 48.4 %attend_more.2 = (f32[4096,128]{1,0:T(8,128)S(1)}, f32[4096,128]{1,0:T(8,128)S(1)}) custom-call(bf16[4096,128]{1,0:T(8,128)(2,1)S(1)} %pad_maximum_fusion.q_ref, bf16[2,512,128]{2,1,0:T(8,128)(2,1)S(1)} %collective-permute-done.8.refs_0_, bf16[2,512,128]{2,1,0:T(8,128)(2,1)S(1)} %collective-permute-done.9.refs_1_, ...), custom_call_target="tpu_custom_call", output_to_operand_aliasing={{0}: (3, {}), {1}: (4, {})} | custom-call | flops 4294967296 | bytes 8388608 | tf_op jit(solution)/shard_map/attend_more/pallas_call | solution.py:166
  122.8 48.5 %attend_more.3 = (f32[4096,128]{1,0:T(8,128)S(1)}, f32[4096,128]{1,0:T(8,128)S(1)}) custom-call(bf16[4096,128]{1,0:T(8,128)(2,1)S(1)} %pad_maximum_fusion.q_ref, bf16[2,512,128]{2,1,0:T(8,128)(2,1)S(1)} %collective-permute-done.6.refs_0_, bf16[2,512,128]{2,1,0:T(8,128)(2,1)S(1)} %collective-permute-done.7.refs_1_, ...), custom_call_target="tpu_custom_call", output_to_operand_aliasing={{0}: (3, {}), {1}: (4, {})} | custom-call | flops 4294967296 | bytes 8388608 | tf_op jit(solution)/shard_map/attend_more/pallas_call | solution.py:166
  171.3 58.0 %attend_last.1 = (bf16[4096,128]{1,0:T(8,128)(2,1)S(1)}, f32[8,4096]{1,0:T(8,128)S(1)}) custom-call(bf16[4096,128]{1,0:T(8,128)(2,1)S(1)} %pad_maximum_fusion.q_ref, bf16[2,512,128]{2,1,0:T(8,128)(2,1)S(1)} %collective-permute-done.3.refs_0_, bf16[2,512,128]{2,1,0:T(8,128)(2,1)S(1)} %collective-permute-done.4.refs_1_, ...), custom_call_target="tpu_custom_call" | custom-call | flops 6442450944 | bytes 8388608 | tf_op jit(solution)/shard_map/attend_last/pallas_call | solution.py:166
  230.3 1.5 collective-permute-done.11.b_lse
  233.1 1.3 collective-permute-start.12
  234.7 13.0 %collective-permute-done.13.b_lse = f32[8,2048]{1,0:T(8,128)S(1)} collective-permute-done((f32[8,2048]{1,0:T(8,128)S(1)}, f32[8,2048]{1,0:T(8,128)S(1)}, u32[]{:S(2)}, u32[]{:S(2)}) %collective-permute-start.13) | collective-permute-done | bytes 65568 | tf_op jit(solution)/shard_map/ppermute | solution.py:313
  249.0 1.5 collective-permute-start.16
  250.5 1.5 collective-permute-done.16
  252.0 2.3 fusion.1
  255.2 41.1 %all_to_all.9 = bf16[32,16,1280]{2,1,0:T(8,128)(2,1)S(1)} all-to-all(bf16[32,16,1280]{2,1,0:T(8,128)(2,1)S(1)} %bitcast.35), channel_id=1, replica_groups=mesh['xh'=2,'y'=4,'z'=8,'xl'=2,'c'=2] {'z','xl','c'}, dimensions={0} | all-to-all | bytes 2621440 | tf_op jit(solution)/shard_map/all_to_all | solution.py:326
  296.3 2.7 reshape.52
  (70 shorter events, 20.0 us)
Async XLA Ops:
  6.5 245.5 %all-gather.2.cloned.1.call-start = ((), (), s32[]{:S(2)}) async-start(), calls=%async_computation.1 | async-start | bytes 2949120 | tf_op jit(solution)/shard_map/all_gather | solution.py:296
  6.5 12.0 %copy-start.11 = (bf16[4,128,256]{2,1,0:T(8,128)(2,1)S(1)}, bf16[4,128,256]{2,1,0:T(8,128)(2,1)}, u32[]{:S(2)}) copy-start(bf16[4,128,256]{2,1,0:T(8,128)(2,1)} %param.7) | copy-start | bytes 786436
  7.8 19.8 %copy-start = (bf16[512,1024]{1,0:T(8,128)(2,1)S(1)}, bf16[512,1024]{1,0:T(8,128)(2,1)}, u32[]{:S(2)}) copy-start(bf16[512,1024]{1,0:T(8,128)(2,1)} %k_ref.1) | copy-start | bytes 3145732
  7.8 19.8 %copy-start.1 = (bf16[512,1024]{1,0:T(8,128)(2,1)S(1)}, bf16[512,1024]{1,0:T(8,128)(2,1)}, u32[]{:S(2)}) copy-start(bf16[512,1024]{1,0:T(8,128)(2,1)} %v_ref.1) | copy-start | bytes 3145732
  7.8 4.4 %collective-permute-start.14 = (bf16[2,160,256]{2,1,0:T(8,128)(2,1)S(1)}, bf16[2,160,256]{2,1,0:T(8,128)(2,1)S(1)}, u32[]{:S(2)}, u32[]{:S(2)}) collective-permute-start(bf16[2,160,256]{2,1,0:T(8,128)(2,1)S(1)} %get-tuple-element.47), channel_id=1, source_target_pairs={{0,1},{1,0},{2,3},{3,2},{4,5},{5,4},{6,7},{7,6},{8,9},{9,8},{10,11... | collective-permute-start | bytes 491528 | tf_op jit(solution)/shard_map/ppermute | solution.py:288
  12.2 5.5 %collective-permute-start.15 = (bf16[2,160,256]{2,1,0:T(8,128)(2,1)S(1)}, bf16[2,160,256]{2,1,0:T(8,128)(2,1)S(1)}, u32[]{:S(2)}, u32[]{:S(2)}) collective-permute-start(bf16[2,160,256]{2,1,0:T(8,128)(2,1)S(1)} %get-tuple-element.46), channel_id=1, source_target_pairs={{0,2},{2,0},{1,3},{3,1},{4,6},{6,4},{5,7},{7,5},{8,10},{10,8},{9,1... | collective-permute-start | bytes 491528 | tf_op jit(solution)/shard_map/ppermute | solution.py:293
  18.7 6.8 %collective-permute-start = (bf16[1024,128]{1,0:T(8,128)(2,1)S(1)}, bf16[1024,128]{1,0:T(8,128)(2,1)}, u32[]{:S(2)}, u32[]{:S(2)}) collective-permute-start(bf16[1024,128]{1,0:T(8,128)(2,1)S(1)} %bitcast.31), channel_id=1, source_target_pairs={{0,2},{2,0},{1,3},{3,1},{4,6},{6,4},{5,7},{7,5},{8,10},{10,8},{9,1... | collective-permute-start | bytes 786440 | tf_op jit(solution)/shard_map/ppermute | solution.py:276
  19.1 29.4 %collective-permute-start.1 = (bf16[1024,128]{1,0:T(8,128)(2,1)S(1)}, bf16[1024,128]{1,0:T(8,128)(2,1)}, u32[]{:S(2)}, u32[]{:S(2)}) collective-permute-start(bf16[1024,128]{1,0:T(8,128)(2,1)S(1)} %bitcast.32), channel_id=1, source_target_pairs={{0,1},{1,0},{2,3},{3,2},{4,5},{5,4},{6,7},{7,6},{8,9},{9,8},{10,11... | collective-permute-start | bytes 786440 | tf_op jit(solution)/shard_map/ppermute | solution.py:277
  25.5 23.8 %collective-permute-start.2 = (bf16[1024,128]{1,0:T(8,128)(2,1)}, bf16[1024,128]{1,0:T(8,128)(2,1)}, u32[]{:S(2)}, u32[]{:S(2)}) collective-permute-start(bf16[1024,128]{1,0:T(8,128)(2,1)} %collective-permute-done), channel_id=1, source_target_pairs={{0,1},{1,0},{2,3},{3,2},{4,5},{5,4},{6,7},{7,6},{8,9},{9,8},{10,11... | collective-permute-start | bytes 786440 | tf_op jit(solution)/shard_map/ppermute | solution.py:278
  31.0 17.5 %copy-start.7 = (bf16[2,512,128]{2,1,0:T(8,128)(2,1)S(1)}, bf16[2,512,128]{2,1,0:T(8,128)(2,1)}, u32[]{:S(2)}) copy-start(bf16[2,512,128]{2,1,0:T(8,128)(2,1)} %copy-done.6) | copy-start | bytes 786436
  31.0 18.3 %copy-start.5 = (bf16[2,512,128]{2,1,0:T(8,128)(2,1)S(1)}, bf16[2,512,128]{2,1,0:T(8,128)(2,1)}, u32[]{:S(2)}) copy-start(bf16[2,512,128]{2,1,0:T(8,128)(2,1)} %copy-done.4) | copy-start | bytes 786436
  31.0 140.3 %collective-permute-start.3 = (bf16[2,512,128]{2,1,0:T(8,128)(2,1)S(1)}, bf16[2,512,128]{2,1,0:T(8,128)(2,1)S(1)}, u32[]{:S(2)}, u32[]{:S(2)}) collective-permute-start(bf16[2,512,128]{2,1,0:T(8,128)(2,1)S(1)} %get-tuple-element.25), channel_id=1, source_target_pairs={{0,12},{4,16},{8,20},{12,24},{16,28},{20,0},{24,4},{28,8},{1,13},{... | collective-permute-start | bytes 786440 | tf_op jit(solution)/shard_map/ppermute | solution.py:283
  33.6 137.7 %collective-permute-start.4 = (bf16[2,512,128]{2,1,0:T(8,128)(2,1)S(1)}, bf16[2,512,128]{2,1,0:T(8,128)(2,1)S(1)}, u32[]{:S(2)}, u32[]{:S(2)}) collective-permute-start(bf16[2,512,128]{2,1,0:T(8,128)(2,1)S(1)} %get-tuple-element.26), channel_id=1, source_target_pairs={{0,20},{4,24},{8,28},{12,0},{16,4},{20,8},{24,12},{28,16},{1,21},{... | collective-permute-start | bytes 786440 | tf_op jit(solution)/shard_map/ppermute | solution.py:283
  35.7 135.6 %collective-permute-start.5 = (bf16[2,512,128]{2,1,0:T(8,128)(2,1)S(1)}, bf16[2,512,128]{2,1,0:T(8,128)(2,1)S(1)}, u32[]{:S(2)}, u32[]{:S(2)}) collective-permute-start(bf16[2,512,128]{2,1,0:T(8,128)(2,1)S(1)} %get-tuple-element.27), channel_id=1, source_target_pairs={{0,16},{4,20},{8,24},{12,28},{16,0},{20,4},{24,8},{28,12},{1,17},{... | collective-permute-start | bytes 786440 | tf_op jit(solution)/shard_map/ppermute | solution.py:283
  48.5 21.1 %collective-permute-start.8 = (bf16[2,512,128]{2,1,0:T(8,128)(2,1)S(1)}, bf16[2,512,128]{2,1,0:T(8,128)(2,1)S(1)}, u32[]{:S(2)}, u32[]{:S(2)}) collective-permute-start(bf16[2,512,128]{2,1,0:T(8,128)(2,1)S(1)} %copy-done.7), channel_id=1, source_target_pairs={{0,4},{4,8},{8,12},{12,16},{16,20},{20,24},{24,28},{28,0},{1,5},{5... | collective-permute-start | bytes 786440 | tf_op jit(solution)/shard_map/ppermute | solution.py:283
  49.3 21.9 %collective-permute-start.9 = (bf16[2,512,128]{2,1,0:T(8,128)(2,1)S(1)}, bf16[2,512,128]{2,1,0:T(8,128)(2,1)S(1)}, u32[]{:S(2)}, u32[]{:S(2)}) collective-permute-start(bf16[2,512,128]{2,1,0:T(8,128)(2,1)S(1)} %copy-done.5), channel_id=1, source_target_pairs={{0,28},{4,0},{8,4},{12,8},{16,12},{20,16},{24,20},{28,24},{1,29},{... | collective-permute-start | bytes 786440 | tf_op jit(solution)/shard_map/ppermute | solution.py:283
  53.6 16.0 %copy-start.3 = (bf16[2,512,128]{2,1,0:T(8,128)(2,1)S(1)}, bf16[2,512,128]{2,1,0:T(8,128)(2,1)}, u32[]{:S(2)}) copy-start(bf16[2,512,128]{2,1,0:T(8,128)(2,1)} %copy-done.2) | copy-start | bytes 786436
  69.6 53.2 %collective-permute-start.6 = (bf16[2,512,128]{2,1,0:T(8,128)(2,1)S(1)}, bf16[2,512,128]{2,1,0:T(8,128)(2,1)S(1)}, u32[]{:S(2)}, u32[]{:S(2)}) collective-permute-start(bf16[2,512,128]{2,1,0:T(8,128)(2,1)S(1)} %copy-done.3), channel_id=1, source_target_pairs={{0,8},{4,12},{8,16},{12,20},{16,24},{20,28},{24,0},{28,4},{1,9},{5... | collective-permute-start | bytes 786440 | tf_op jit(solution)/shard_map/ppermute | solution.py:283
  71.2 51.6 %collective-permute-start.7 = (bf16[2,512,128]{2,1,0:T(8,128)(2,1)S(1)}, bf16[2,512,128]{2,1,0:T(8,128)(2,1)S(1)}, u32[]{:S(2)}, u32[]{:S(2)}) collective-permute-start(bf16[2,512,128]{2,1,0:T(8,128)(2,1)S(1)} %get-tuple-element.29), channel_id=1, source_target_pairs={{0,24},{4,28},{8,0},{12,4},{16,8},{20,12},{24,16},{28,20},{1,25},{... | collective-permute-start | bytes 786440 | tf_op jit(solution)/shard_map/ppermute | solution.py:283
  229.4 2.4 collective-permute-start.10
  230.2 1.6 collective-permute-start.11
  233.1 14.6 %collective-permute-start.12 = (bf16[2048,128]{1,0:T(8,128)(2,1)S(1)}, bf16[2048,128]{1,0:T(8,128)(2,1)S(1)}, u32[]{:S(2)}, u32[]{:S(2)}) collective-permute-start(bf16[2048,128]{1,0:T(8,128)(2,1)S(1)} %get-tuple-element.43.a_ref), channel_id=1, source_target_pairs={{0,2},{2,0},{1,3},{3,1},{4,6},{6,4},{5,7},{7,5},{8,10},{10,8},{9,1... | collective-permute-start | bytes 1572872 | tf_op jit(solution)/shard_map/ppermute | solution.py:313
  234.4 13.3 %collective-permute-start.13 = (f32[8,2048]{1,0:T(8,128)S(1)}, f32[8,2048]{1,0:T(8,128)S(1)}, u32[]{:S(2)}, u32[]{:S(2)}) collective-permute-start(f32[8,2048]{1,0:T(8,128)S(1)} %get-tuple-element.44.a_lse), channel_id=1, source_target_pairs={{0,2},{2,0},{1,3},{3,1},{4,6},{6,4},{5,7},{7,5},{8,10},{10,8},{9,1... | collective-permute-start | bytes 196616 | tf_op jit(solution)/shard_map/ppermute | solution.py:313
  249.0 3.0 collective-permute-start.16
  (7 other events, 11.4 us)
Sparse Core Ops, SparseCore 0:
  18.7 64.7 all-gather.1
